TPU v7x, 256 devices: a whole 4x4x8 slice. The times are simulated.
256 devices in a mesh: seq: 32 (over y, x, core), chan: 8 (over z).
Axes of the slice: x: 4, y: 4, z: 8, core: 2. Of those that a mesh axis runs over, the one named last changes fastest.
Arguments:
- q_proj: bfloat16 [32768, 8192], P('seq', 'chan'), may hold values from -6 to 6
- k_proj: bfloat16 [32768, 8192], P('seq', 'chan'), may hold values from -6 to 6
- v_proj: bfloat16 [32768, 8192], P('seq', 'chan'), may hold values from -6 to 6
- short_filter: float32 [3, 3, 8192], P(None, None, 'chan'), may hold values from -3 to 3
- decay_rate: float32 [64, 16], P('chan'), may hold values from 0 to 1, as said below
- residue: float32 [64, 16], P('chan'), may hold values from -1 to 1
Outputs:
- regrouped: bfloat16 [32, 8, 32, 32768], P('seq', None, None, 'chan')
Inputs may be any that keep to these rules, and one draw needn't show every extreme that they name: `decay_rate`: positive rates.
All inputs are finite; a program needn't handle non-finite values.
Results may differ from a plain program's by a relative error of at most 0.012.
Values may be sent and summed in bfloat16 or wider, within the bound.
A program may use at most 128 MiB of HBM per device.

v0:
```python
import jax
import jax.numpy as jnp
from jax import lax
from jax.sharding import PartitionSpec as P


def passed_along(block, axis, distance):
    devices = range(lax.axis_size(axis))
    route = [(i - distance, i) for i in devices if i - distance in devices]
    return lax.ppermute(block, axis, route)


def causal_short(current, rim, taps):
    extended = jnp.concatenate([rim, current], axis=0).astype(jnp.float32)
    return taps[0] * extended[2:] + taps[1] * extended[1:-1] + taps[2] * extended[:-2]


def modal_conv(gated, decays, residues, block_len, initial):
    length, head_count, channels = gated.shape
    block_count = length // block_len
    offsets = jnp.arange(block_len, dtype=jnp.float32)
    distance = offsets[:, None] - offsets[None, :]
    lagged = jnp.maximum(distance, 0.0)
    summed = jnp.sum(
        residues[:, None, None, :] * jnp.exp(-decays[:, None, None, :] * lagged[None, :, :, None]),
        axis=3,
    )
    toeplitz = jnp.where(distance[None] >= 0.0, summed, jnp.float32(0.0))
    from_state = residues[:, None, :] * jnp.exp(
        -decays[:, None, :] * (offsets + 1.0)[None, :, None]
    )
    kernel_aug = jnp.concatenate([toeplitz, from_state], axis=2)
    into_state = jnp.exp(-decays[:, :, None] * (block_len - 1.0 - offsets)[None, None, :])
    carry_decay = jnp.exp(-decays * block_len)[:, :, None]
    segments = gated.reshape(block_count, block_len, head_count, channels)

    def advance(carry_state, segment):
        values = segment.astype(jnp.float32)
        stacked = jnp.concatenate([values, carry_state.transpose(1, 0, 2)], axis=0)
        piece = jnp.einsum("htk,khc->thc", kernel_aug, stacked, precision=lax.Precision.HIGHEST)
        carry_state = carry_decay * carry_state + jnp.einsum(
            "hrs,shc->hrc", into_state, values, precision=lax.Precision.HIGHEST
        )
        return (carry_state, piece)

    last_state, pieces = lax.scan(advance, initial, segments)
    return (pieces.reshape(length, head_count, channels), last_state)


def per_device(q_proj, k_proj, v_proj, short_filter, decay_rate, residue):
    rows_here, group_width = q_proj.shape
    head_count, mode_count = decay_rate.shape
    head_width = group_width // head_count
    seq_count = lax.axis_size("seq")
    sub_width = group_width // seq_count
    rims = passed_along((q_proj[-2:], k_proj[-2:], v_proj[-2:]), "seq", 1)
    query_mix = causal_short(q_proj, rims[0], short_filter[0]).astype(jnp.bfloat16)
    gated = (
        causal_short(k_proj, rims[1], short_filter[1])
        * causal_short(v_proj, rims[2], short_filter[2])
    ).astype(jnp.bfloat16)
    gated_heads = gated.reshape(rows_here, head_count, head_width)
    offsets = jnp.arange(rows_here, dtype=jnp.float32)
    weighting = jnp.exp(-decay_rate[:, :, None] * (rows_here - 1.0 - offsets)[None, None, :])
    state_out = jnp.einsum(
        "hrs,shc->hrc", weighting, gated_heads.astype(jnp.float32), precision=lax.Precision.HIGHEST
    )
    shard_decay = jnp.exp(-decay_rate * rows_here)[:, :, None]

    def forward(counter, incoming):
        return passed_along(shard_decay * incoming + state_out, "seq", 1)

    state_in = lax.fori_loop(0, seq_count - 1, forward, jnp.zeros_like(state_out))
    convolved, _ = modal_conv(gated_heads, decay_rate, residue, min(128, rows_here), state_in)
    mixed = (query_mix.astype(jnp.float32) * convolved.reshape(rows_here, group_width)).astype(
        jnp.bfloat16
    )
    blocks = mixed.T.reshape(seq_count, 1, sub_width, rows_here)
    return lax.all_to_all(
        lax.all_to_all(blocks, "seq", split_axis=0, concat_axis=3, tiled=True),
        "chan",
        split_axis=3,
        concat_axis=1,
        tiled=True,
    )


def solution(mesh):
    in_specs = (
        P("seq", "chan"),
        P("seq", "chan"),
        P("seq", "chan"),
        P(None, None, "chan"),
        P("chan", None),
        P("chan", None),
    )
    out_specs = P("seq", None, None, "chan")
    return jax.shard_map(
        per_device, mesh=mesh, in_specs=in_specs, out_specs=out_specs, check_vma=False
    )
```

profile of v0, /device:TPU:1, one launch (start us, length us, event | category | flops | bytes accessed | tf_op | source)
XLA Modules:
  0.0 663.1 jit_solution(15644092054516402645)
XLA Ops:
  0.7 4.5 collective-permute-start.3
  8.6 3.5 collective-permute-start.1
  13.8 3.5 multiply_reduce_fusion
  18.7 2.4 maximum_convert_fusion.1
  21.7 2.9 fusion.34
  24.6 3.5 fusion.22
  30.1 213.2 %while.23 = (s32[]{:T(128)}, f32[8,16,128]{2,1,0:T(8,128)S(1)}, f32[8,16,1]{1,0,2:T(8,128)S(1)}, f32[8,16,128]{2,1,0:T(8,128)S(1)}, s32[]{:T(128)}) while((s32[]{:T(128)}, f32[8,16,128]{2,1,0:T(8,128)S(1)}, f32[8,16,1]{1,0,2:T(8,128)S(1)}, f32[8,16,128]{2,1,0:T(8,128)S(1)}, s32[]{:T(128)}) %tuple.47), condition=%wide.region_1.0_spmd, body=%wide.region_0.0_spmd.sunk | while | flops 32770 | bytes 459365 | solution.py:73
  33.5 4.3 collective-permute-start
  39.2 4.3 collective-permute-start
  44.8 4.3 collective-permute-start
  50.5 4.3 collective-permute-start
  56.2 4.3 collective-permute-start
  61.9 4.3 collective-permute-start
  67.5 4.3 collective-permute-start
  73.2 4.3 collective-permute-start
  78.9 4.3 collective-permute-start
  84.5 4.3 collective-permute-start
  90.2 4.3 collective-permute-start
  95.9 6.0 collective-permute-start
  103.3 6.4 collective-permute-start
  111.1 6.4 collective-permute-start
  118.8 6.4 collective-permute-start
  126.6 6.4 collective-permute-start
  134.4 6.4 collective-permute-start
  142.2 6.4 collective-permute-start
  150.0 6.4 collective-permute-start
  157.8 6.4 collective-permute-start
  165.5 6.4 collective-permute-start
  173.3 6.4 collective-permute-start
  181.1 6.4 collective-permute-start
  188.9 6.4 collective-permute-start
  196.7 6.4 collective-permute-start
  204.4 6.4 collective-permute-start
  212.2 6.4 collective-permute-start
  220.0 6.4 collective-permute-start
  227.8 6.4 collective-permute-start
  235.6 6.4 collective-permute-start
  243.3 34.8 %while.24 = (s32[]{:T(128)}, f32[8,16,128]{2,1,0:T(8,128)S(1)}, f32[8,128,8,128]{3,2,1,0:T(8,128)}, f32[8,16,1]{1,0,2:T(8,128)S(1)}, bf16[8,128,8,128]{3,2,1,0:T...) while((s32[]{:T(128)}, f32[8,16,128]{2,1,0:T(8,128)S(1)}, ...), condition=%wide.region_4.5_spmd.clone, body=%wide.region_3.4_spmd.clone.sunk | while | flops 251985920 | bytes 5506669 | solution.py:46
  278.1 2.4 maximum_convert_fusion
  282.7 2.6 copy.30
  285.3 60.0 %all_to_all.36 = bf16[32,1,32,1024]{3,2,1,0:T(8,128)(2,1)S(1)} all-to-all(bf16[32,1,32,1024]{3,2,1,0:T(8,128)(2,1)} %bitcast.90), channel_id=1, replica_groups=mesh['seq'=32,'chan'=8] {'seq'}, dimensions={0} | all-to-all | bytes 4194304 | tf_op jit(solution)/shard_map/all_to_all | solution.py:80
  345.4 25.2 %copy.33 = bf16[1,1,32,32768]{2,1,0,3:T(2,128)(2,1)} copy(bf16[1,1,32,32768]{3,2,1,0:T(8,128)(2,1)S(1)} %bitcast.88) | data formatting | bytes 4194304 | tf_op jit(solution)/shard_map/all_to_all | solution.py:80
  371.1 179.1 %reduce = bf16[32768,32]{1,0:T(8,128)(2,1)} reduce(bf16[32768,1,1,32]{3,2,1,0:T(2,128)(2,1)} %bitcast.87, bf16[]{:T(256)} %broadcast.37), dimensions={1,2}, to_apply=%bitcast.63.reduce_sub_computation | reduce | bytes 4194306
  550.2 10.1 %reshape.74 = bf16[8,2,65536]{2,1,0:T(2,128)(2,1)S(1)} reshape(bf16[32768,32]{1,0:T(8,128)(2,1)} %reduce) | data formatting | bytes 4194304
  560.4 58.4 %all_to_all.37 = bf16[8,2,65536]{2,1,0:T(2,128)(2,1)} all-to-all(bf16[8,2,65536]{2,1,0:T(2,128)(2,1)S(1)} %reshape.74), channel_id=1, replica_groups=mesh['seq'=32,'chan'=8] {'chan'}, dimensions={0} | all-to-all | bytes 4194304 | tf_op jit(solution)/shard_map/all_to_all | solution.py:79
  618.7 10.6 %reshape.75 = bf16[32768,1,1,32]{3,2,1,0:T(2,128)(2,1)} reshape(bf16[8,2,65536]{2,1,0:T(2,128)(2,1)} %all_to_all.37) | data formatting | bytes 4194304
  629.4 30.0 %copy.34 = bf16[1,1,32,32768]{3,2,1,0:T(8,128)(2,1)S(1)} copy(bf16[1,1,32,32768]{2,1,0,3:T(2,128)(2,1)} %bitcast.86) | data formatting | bytes 4194304 | tf_op jit(solution)/shard_map/all_to_all | solution.py:79
  660.6 2.5 copy.35
  (141 shorter events, 93.2 us)
Async XLA Ops:
  0.7 20.3 %collective-permute-start.3 = (bf16[2,1024]{1,0:T(2,128)(2,1)S(1)}, bf16[2,1024]{1,0:T(2,128)(2,1)S(1)}, u32[]{:S(2)}, u32[]{:S(2)}) collective-permute-start(bf16[2,1024]{1,0:T(2,128)(2,1)S(1)} %slice.99), channel_id=1, source_target_pairs={{0,8},{8,16},{16,24},{24,32},{32,40},{40,48},{48,56},{56,64},{64,7... | collective-permute-start | bytes 12296 | tf_op jit(solution)/shard_map/ppermute | solution.py:10
  6.0 12.7 %collective-permute-start.2 = (bf16[2,1024]{1,0:T(2,128)(2,1)S(1)}, bf16[2,1024]{1,0:T(2,128)(2,1)S(1)}, u32[]{:S(2)}, u32[]{:S(2)}) collective-permute-start(bf16[2,1024]{1,0:T(2,128)(2,1)S(1)} %slice.92), channel_id=1, source_target_pairs={{0,8},{8,16},{16,24},{24,32},{32,40},{40,48},{48,56},{56,64},{64,7... | collective-permute-start | bytes 12296 | tf_op jit(solution)/shard_map/ppermute | solution.py:10
  8.6 269.5 %collective-permute-start.1 = (bf16[2,1024]{1,0:T(2,128)(2,1)S(1)}, bf16[2,1024]{1,0:T(2,128)(2,1)S(1)}, u32[]{:S(2)}, u32[]{:S(2)}) collective-permute-start(bf16[2,1024]{1,0:T(2,128)(2,1)S(1)} %slice.85), channel_id=1, source_target_pairs={{0,8},{8,16},{16,24},{24,32},{32,40},{40,48},{48,56},{56,64},{64,7... | collective-permute-start | bytes 12296 | tf_op jit(solution)/shard_map/ppermute | solution.py:10
  18.6 2.4 copy-start.1
  30.2 3.2 collective-permute-start
  33.5 5.6 collective-permute-start
  39.2 5.6 collective-permute-start
  44.8 5.6 collective-permute-start
  50.5 5.6 collective-permute-start
  56.2 5.6 collective-permute-start
  61.9 5.6 collective-permute-start
  67.5 5.6 collective-permute-start
  73.2 5.6 collective-permute-start
  78.9 5.6 collective-permute-start
  84.5 5.6 collective-permute-start
  90.2 5.6 collective-permute-start
  95.9 7.3 %collective-permute-start = (f32[8,16,128]{2,1,0:T(8,128)S(1)}, f32[8,16,128]{2,1,0:T(8,128)S(1)}, u32[]{:S(2)}, u32[]{:S(2)}) collective-permute-start(f32[8,16,128]{2,1,0:T(8,128)S(1)} %multiply_add_fusion.2), channel_id=1, source_target_pairs={{0,8},{8,16},{16,24},{24,32},{32,40},{40,48},{48,56},{56,64},{64,7... | collective-permute-start | bytes 196616 | tf_op jit(solution)/shard_map/while/body/eval_jaxpr/ppermute | solution.py:10
  103.3 7.7 %collective-permute-start = (f32[8,16,128]{2,1,0:T(8,128)S(1)}, f32[8,16,128]{2,1,0:T(8,128)S(1)}, u32[]{:S(2)}, u32[]{:S(2)}) collective-permute-start(f32[8,16,128]{2,1,0:T(8,128)S(1)} %multiply_add_fusion.2), channel_id=1, source_target_pairs={{0,8},{8,16},{16,24},{24,32},{32,40},{40,48},{48,56},{56,64},{64,7... | collective-permute-start | bytes 196616 | tf_op jit(solution)/shard_map/while/body/eval_jaxpr/ppermute | solution.py:10
  111.1 7.7 %collective-permute-start = (f32[8,16,128]{2,1,0:T(8,128)S(1)}, f32[8,16,128]{2,1,0:T(8,128)S(1)}, u32[]{:S(2)}, u32[]{:S(2)}) collective-permute-start(f32[8,16,128]{2,1,0:T(8,128)S(1)} %multiply_add_fusion.2), channel_id=1, source_target_pairs={{0,8},{8,16},{16,24},{24,32},{32,40},{40,48},{48,56},{56,64},{64,7... | collective-permute-start | bytes 196616 | tf_op jit(solution)/shard_map/while/body/eval_jaxpr/ppermute | solution.py:10
  118.8 7.7 %collective-permute-start = (f32[8,16,128]{2,1,0:T(8,128)S(1)}, f32[8,16,128]{2,1,0:T(8,128)S(1)}, u32[]{:S(2)}, u32[]{:S(2)}) collective-permute-start(f32[8,16,128]{2,1,0:T(8,128)S(1)} %multiply_add_fusion.2), channel_id=1, source_target_pairs={{0,8},{8,16},{16,24},{24,32},{32,40},{40,48},{48,56},{56,64},{64,7... | collective-permute-start | bytes 196616 | tf_op jit(solution)/shard_map/while/body/eval_jaxpr/ppermute | solution.py:10
  126.6 7.7 %collective-permute-start = (f32[8,16,128]{2,1,0:T(8,128)S(1)}, f32[8,16,128]{2,1,0:T(8,128)S(1)}, u32[]{:S(2)}, u32[]{:S(2)}) collective-permute-start(f32[8,16,128]{2,1,0:T(8,128)S(1)} %multiply_add_fusion.2), channel_id=1, source_target_pairs={{0,8},{8,16},{16,24},{24,32},{32,40},{40,48},{48,56},{56,64},{64,7... | collective-permute-start | bytes 196616 | tf_op jit(solution)/shard_map/while/body/eval_jaxpr/ppermute | solution.py:10
  134.4 7.7 %collective-permute-start = (f32[8,16,128]{2,1,0:T(8,128)S(1)}, f32[8,16,128]{2,1,0:T(8,128)S(1)}, u32[]{:S(2)}, u32[]{:S(2)}) collective-permute-start(f32[8,16,128]{2,1,0:T(8,128)S(1)} %multiply_add_fusion.2), channel_id=1, source_target_pairs={{0,8},{8,16},{16,24},{24,32},{32,40},{40,48},{48,56},{56,64},{64,7... | collective-permute-start | bytes 196616 | tf_op jit(solution)/shard_map/while/body/eval_jaxpr/ppermute | solution.py:10
  142.2 7.7 %collective-permute-start = (f32[8,16,128]{2,1,0:T(8,128)S(1)}, f32[8,16,128]{2,1,0:T(8,128)S(1)}, u32[]{:S(2)}, u32[]{:S(2)}) collective-permute-start(f32[8,16,128]{2,1,0:T(8,128)S(1)} %multiply_add_fusion.2), channel_id=1, source_target_pairs={{0,8},{8,16},{16,24},{24,32},{32,40},{40,48},{48,56},{56,64},{64,7... | collective-permute-start | bytes 196616 | tf_op jit(solution)/shard_map/while/body/eval_jaxpr/ppermute | solution.py:10
  150.0 7.7 %collective-permute-start = (f32[8,16,128]{2,1,0:T(8,128)S(1)}, f32[8,16,128]{2,1,0:T(8,128)S(1)}, u32[]{:S(2)}, u32[]{:S(2)}) collective-permute-start(f32[8,16,128]{2,1,0:T(8,128)S(1)} %multiply_add_fusion.2), channel_id=1, source_target_pairs={{0,8},{8,16},{16,24},{24,32},{32,40},{40,48},{48,56},{56,64},{64,7... | collective-permute-start | bytes 196616 | tf_op jit(solution)/shard_map/while/body/eval_jaxpr/ppermute | solution.py:10
  157.8 7.7 %collective-permute-start = (f32[8,16,128]{2,1,0:T(8,128)S(1)}, f32[8,16,128]{2,1,0:T(8,128)S(1)}, u32[]{:S(2)}, u32[]{:S(2)}) collective-permute-start(f32[8,16,128]{2,1,0:T(8,128)S(1)} %multiply_add_fusion.2), channel_id=1, source_target_pairs={{0,8},{8,16},{16,24},{24,32},{32,40},{40,48},{48,56},{56,64},{64,7... | collective-permute-start | bytes 196616 | tf_op jit(solution)/shard_map/while/body/eval_jaxpr/ppermute | solution.py:10
  165.5 7.7 %collective-permute-start = (f32[8,16,128]{2,1,0:T(8,128)S(1)}, f32[8,16,128]{2,1,0:T(8,128)S(1)}, u32[]{:S(2)}, u32[]{:S(2)}) collective-permute-start(f32[8,16,128]{2,1,0:T(8,128)S(1)} %multiply_add_fusion.2), channel_id=1, source_target_pairs={{0,8},{8,16},{16,24},{24,32},{32,40},{40,48},{48,56},{56,64},{64,7... | collective-permute-start | bytes 196616 | tf_op jit(solution)/shard_map/while/body/eval_jaxpr/ppermute | solution.py:10
  173.3 7.7 %collective-permute-start = (f32[8,16,128]{2,1,0:T(8,128)S(1)}, f32[8,16,128]{2,1,0:T(8,128)S(1)}, u32[]{:S(2)}, u32[]{:S(2)}) collective-permute-start(f32[8,16,128]{2,1,0:T(8,128)S(1)} %multiply_add_fusion.2), channel_id=1, source_target_pairs={{0,8},{8,16},{16,24},{24,32},{32,40},{40,48},{48,56},{56,64},{64,7... | collective-permute-start | bytes 196616 | tf_op jit(solution)/shard_map/while/body/eval_jaxpr/ppermute | solution.py:10
  181.1 7.7 %collective-permute-start = (f32[8,16,128]{2,1,0:T(8,128)S(1)}, f32[8,16,128]{2,1,0:T(8,128)S(1)}, u32[]{:S(2)}, u32[]{:S(2)}) collective-permute-start(f32[8,16,128]{2,1,0:T(8,128)S(1)} %multiply_add_fusion.2), channel_id=1, source_target_pairs={{0,8},{8,16},{16,24},{24,32},{32,40},{40,48},{48,56},{56,64},{64,7... | collective-permute-start | bytes 196616 | tf_op jit(solution)/shard_map/while/body/eval_jaxpr/ppermute | solution.py:10
  188.9 7.7 %collective-permute-start = (f32[8,16,128]{2,1,0:T(8,128)S(1)}, f32[8,16,128]{2,1,0:T(8,128)S(1)}, u32[]{:S(2)}, u32[]{:S(2)}) collective-permute-start(f32[8,16,128]{2,1,0:T(8,128)S(1)} %multiply_add_fusion.2), channel_id=1, source_target_pairs={{0,8},{8,16},{16,24},{24,32},{32,40},{40,48},{48,56},{56,64},{64,7... | collective-permute-start | bytes 196616 | tf_op jit(solution)/shard_map/while/body/eval_jaxpr/ppermute | solution.py:10
  196.7 7.7 %collective-permute-start = (f32[8,16,128]{2,1,0:T(8,128)S(1)}, f32[8,16,128]{2,1,0:T(8,128)S(1)}, u32[]{:S(2)}, u32[]{:S(2)}) collective-permute-start(f32[8,16,128]{2,1,0:T(8,128)S(1)} %multiply_add_fusion.2), channel_id=1, source_target_pairs={{0,8},{8,16},{16,24},{24,32},{32,40},{40,48},{48,56},{56,64},{64,7... | collective-permute-start | bytes 196616 | tf_op jit(solution)/shard_map/while/body/eval_jaxpr/ppermute | solution.py:10
  204.4 7.7 %collective-permute-start = (f32[8,16,128]{2,1,0:T(8,128)S(1)}, f32[8,16,128]{2,1,0:T(8,128)S(1)}, u32[]{:S(2)}, u32[]{:S(2)}) collective-permute-start(f32[8,16,128]{2,1,0:T(8,128)S(1)} %multiply_add_fusion.2), channel_id=1, source_target_pairs={{0,8},{8,16},{16,24},{24,32},{32,40},{40,48},{48,56},{56,64},{64,7... | collective-permute-start | bytes 196616 | tf_op jit(solution)/shard_map/while/body/eval_jaxpr/ppermute | solution.py:10
  212.2 7.7 %collective-permute-start = (f32[8,16,128]{2,1,0:T(8,128)S(1)}, f32[8,16,128]{2,1,0:T(8,128)S(1)}, u32[]{:S(2)}, u32[]{:S(2)}) collective-permute-start(f32[8,16,128]{2,1,0:T(8,128)S(1)} %multiply_add_fusion.2), channel_id=1, source_target_pairs={{0,8},{8,16},{16,24},{24,32},{32,40},{40,48},{48,56},{56,64},{64,7... | collective-permute-start | bytes 196616 | tf_op jit(solution)/shard_map/while/body/eval_jaxpr/ppermute | solution.py:10
  220.0 7.7 %collective-permute-start = (f32[8,16,128]{2,1,0:T(8,128)S(1)}, f32[8,16,128]{2,1,0:T(8,128)S(1)}, u32[]{:S(2)}, u32[]{:S(2)}) collective-permute-start(f32[8,16,128]{2,1,0:T(8,128)S(1)} %multiply_add_fusion.2), channel_id=1, source_target_pairs={{0,8},{8,16},{16,24},{24,32},{32,40},{40,48},{48,56},{56,64},{64,7... | collective-permute-start | bytes 196616 | tf_op jit(solution)/shard_map/while/body/eval_jaxpr/ppermute | solution.py:10
  227.8 7.7 %collective-permute-start = (f32[8,16,128]{2,1,0:T(8,128)S(1)}, f32[8,16,128]{2,1,0:T(8,128)S(1)}, u32[]{:S(2)}, u32[]{:S(2)}) collective-permute-start(f32[8,16,128]{2,1,0:T(8,128)S(1)} %multiply_add_fusion.2), channel_id=1, source_target_pairs={{0,8},{8,16},{16,24},{24,32},{32,40},{40,48},{48,56},{56,64},{64,7... | collective-permute-start | bytes 196616 | tf_op jit(solution)/shard_map/while/body/eval_jaxpr/ppermute | solution.py:10
  235.6 7.7 %collective-permute-start = (f32[8,16,128]{2,1,0:T(8,128)S(1)}, f32[8,16,128]{2,1,0:T(8,128)S(1)}, u32[]{:S(2)}, u32[]{:S(2)}) collective-permute-start(f32[8,16,128]{2,1,0:T(8,128)S(1)} %multiply_add_fusion.2), channel_id=1, source_target_pairs={{0,8},{8,16},{16,24},{24,32},{32,40},{40,48},{48,56},{56,64},{64,7... | collective-permute-start | bytes 196616 | tf_op jit(solution)/shard_map/while/body/eval_jaxpr/ppermute | solution.py:10
  278.1 2.8 copy-start
where the time goes:
time: 666 us; the launch traced here: 663 us
  other arithmetic  197 us (30%)
  starting transfers between devices  180 us (27%)
  blocking collectives  118 us (18%)
  local copies, waits for them, and re-layouts  105 us (16%)
  waiting for transfers between devices  40.5 us (6%)
  matrix products  21.5 us (3%)
    unnamed x2, other arithmetic  182 us
    ppermute x34, starting transfers between devices, passed_along(): return lax.ppermute(block, axis, route)  180 us
    all_to_all x1, blocking collectives, per_device(): lax.all_to_all(blocks, 'seq', split_axis=0, concat_axis=3, tiled=True)  60 us
    all_to_all x1, blocking collectives, per_device(): lax.all_to_all(lax.all_to_all(blocks, 'seq', split_axis=0, concat_axis=3,...  58.4 us
    ppermute x34, waiting for transfers between devices, passed_along(): return lax.ppermute(block, axis, route)  40.5 us
    all_to_all x2, local copies, waits for them, and re-layouts, per_device(): lax.all_to_all(lax.all_to_all(blocks, 'seq', split_axis=0, concat_axis=3,...  32.5 us
    all_to_all x2, local copies, waits for them, and re-layouts, per_device(): lax.all_to_all(blocks, 'seq', split_axis=0, concat_axis=3, tiled=True)  25.4 us
    unnamed x10, local copies, waits for them, and re-layouts  25.2 us
  transfers between devices with their start and end apart: 34, of which 31 were waited for; matrix products, arithmetic and copies ran while one was open for 8% of the time, Pallas kernels for 0%

commit v1 on v0

v1 whole, which is shorter than its diff:
```python
import functools

import jax
import jax.numpy as jnp
from jax import lax
from jax.experimental import pallas as pl
from jax.experimental.pallas import tpu as pltpu
from jax.sharding import PartitionSpec as P

MESH = pl.DeviceIdType.MESH
F32, BF16 = jnp.float32, jnp.bfloat16

ROWS = 1024
HEADS = 8
WIDE = 128
MODES = 16
BLOCK = 128
BLOCKS = ROWS // BLOCK
PAD = 16
NSEQ = 32
NCHAN = 8
SUB = 32
ROW = 8


def split(x):
    high = x.astype(BF16)
    return high, (x - high.astype(F32)).astype(BF16)


def matmul(a, b):
    return jnp.dot(a, b, preferred_element_type=F32)


def start_of(residue, chan):
    place = lax.rem(residue + 4 * lax.rem(chan, 2), 8)
    return 2 * lax.rem(place, 4) + place // 4


def residue_of(start, chan):
    return lax.rem(4 * lax.rem(start, 2) + start // 2 + 4 * lax.rem(chan, 2), 8)


def kernel(
    q_ref, k_ref, v_ref, taps_ref, decay_ref, residue_ref, out_ref,
    q_raw, k_raw, v_raw, rim, gated, q_mix, toeplitz, from_state, into_state,
    decays, part, local, row_in, col_in, col_out, state, mixed, middle,
    load_q, load_k, load_v, rim_send, rim_recv,
    local_send, row_recv, col_send, col_recv, state_send, state_recv,
    a_send, a_recv, b_send, b_recv,
):
    seq, chan = lax.axis_index("seq"), lax.axis_index("chan")
    yy, rr = seq // ROW, lax.rem(seq, ROW)

    barrier = pltpu.get_barrier_semaphore()

    @pl.loop(1, NSEQ)
    def _(i):
        pl.semaphore_signal(
            barrier, inc=1, device_id=(lax.rem(seq + i, NSEQ), chan), device_id_type=MESH
        )

    @pl.loop(1, NCHAN)
    def _(i):
        pl.semaphore_signal(
            barrier, inc=1, device_id=(seq, lax.rem(chan + i, NCHAN)), device_id_type=MESH
        )

    def load(ref, raw, sem, h):
        columns = pl.ds(pl.multiple_of(h * WIDE, WIDE), WIDE)
        return pltpu.make_async_copy(
            ref.at[:, columns], raw.at[h, pl.ds(PAD, ROWS), :], sem.at[h]
        )

    @pl.loop(0, HEADS)
    def _(h):
        load(k_ref, k_raw, load_k, h).start()
        load(v_ref, v_raw, load_v, h).start()

    @pl.loop(0, HEADS)
    def _(h):
        load(q_ref, q_raw, load_q, h).start()

    ones_at = lax.broadcasted_iota(jnp.int32, (MODES, MODES), 0) == lax.broadcasted_iota(
        jnp.int32, (MODES, MODES), 1
    )
    lane = lax.broadcasted_iota(jnp.int32, (MODES, BLOCK), 1)
    causal = lax.broadcasted_iota(jnp.int32, (BLOCK, BLOCK), 0) >= lax.broadcasted_iota(
        jnp.int32, (BLOCK, BLOCK), 1
    )

    def column(row):
        wide = jnp.where(ones_at, jnp.broadcast_to(row, (MODES, MODES)), 0.0)
        return jnp.broadcast_to(jnp.sum(wide, axis=1, keepdims=True), (MODES, WIDE))

    @pl.loop(0, HEADS)
    def _(h):
        rate = column(decay_ref[pl.ds(h, 1), :])
        weight = column(residue_ref[pl.ds(h, 1), :])
        decays[h] = rate
        lag = jnp.where(lane == 0, 0, BLOCK - lane).astype(F32)
        first = jnp.sum(weight * jnp.exp(-rate * lag), axis=0, keepdims=True)
        turned = pltpu.roll(
            jnp.broadcast_to(first, (BLOCK, BLOCK)), 0, 1, stride=1, stride_axis=0
        )
        high, low = split(jnp.where(causal, turned, 0.0))
        toeplitz[h, :, 0:BLOCK] = high
        toeplitz[h, :, BLOCK : 2 * BLOCK] = low
        high, low = split(weight * jnp.exp(-rate * (lane + 1).astype(F32)))
        high, low = high.astype(F32), low.astype(F32)
        rest = jnp.zeros((BLOCK - 3 * MODES, BLOCK), F32)
        from_state[h] = jnp.concatenate([high, low, high, rest], axis=0).T.astype(BF16)
        high, low = split(jnp.exp(-rate * (BLOCK - 1 - lane).astype(F32)))
        into_state[h, 0:MODES] = high
        into_state[h, MODES : 2 * MODES] = low

    pl.semaphore_wait(barrier, NSEQ - 1 + NCHAN - 1)

    after = lax.rem(seq + 1, NSEQ)
    rims = []
    for n, ref in enumerate((k_ref, v_ref, q_ref)):
        copy = pltpu.make_async_remote_copy(
            src_ref=ref.at[pl.ds(ROWS - PAD, PAD), :],
            dst_ref=rim.at[n],
            send_sem=rim_send.at[n],
            recv_sem=rim_recv.at[n],
            device_id=(after, chan),
            device_id_type=MESH,
        )
        copy.start()
        rims.append(copy)

    def short(raw, branch, h, row, count):
        columns = pl.ds(pl.multiple_of(h * WIDE, WIDE), WIDE)
        x = raw[h, pl.ds(row, count + PAD), :].astype(F32)
        y = taps_ref[branch, 0:1, columns] * x
        y = y + taps_ref[branch, 1:2, columns] * pltpu.roll(x, 1, 0)
        y = y + taps_ref[branch, 2:3, columns] * pltpu.roll(x, 2, 0)
        return y[PAD:]

    def gate(h, block):
        row = block * BLOCK
        g = (short(k_raw, 1, h, row, BLOCK) * short(v_raw, 2, h, row, BLOCK)).astype(BF16)
        gated[h, pl.ds(row, BLOCK), :] = g
        both = matmul(into_state[h], g)
        part[h, block] = both[0:MODES] + both[MODES : 2 * MODES]

    @pl.loop(0, HEADS)
    def _(h):
        load(k_ref, k_raw, load_k, h).wait()
        load(v_ref, v_raw, load_v, h).wait()
        for block in range(1, BLOCKS):
            gate(h, block)

    for copy in rims:
        copy.wait()

    def put_rim(raw, n, h):
        columns = pl.ds(pl.multiple_of(h * WIDE, WIDE), WIDE)
        rows = rim[n, :, columns]
        raw[h, 0:PAD, :] = jnp.where(seq > 0, rows, jnp.zeros_like(rows))

    @pl.loop(0, HEADS)
    def _(h):
        put_rim(k_raw, 0, h)
        put_rim(v_raw, 1, h)
        gate(h, 0)
        step = jnp.exp(decays[h] * -float(BLOCK))
        total = part[h, 0]
        for block in range(1, BLOCKS):
            total = step * total + part[h, block]
        local[h] = total

        @pl.when(h == rr)
        def _():
            row_in[rr] = total

        @pl.when(h != rr)
        def _():
            pltpu.make_async_remote_copy(
                src_ref=local.at[h],
                dst_ref=row_in.at[rr],
                send_sem=local_send,
                recv_sem=row_recv,
                device_id=(yy * ROW + h, chan),
                device_id_type=MESH,
            ).start()

    first = start_of(rr, chan)

    def query(i):
        h = lax.rem(first + i, HEADS)
        load(q_ref, q_raw, load_q, h).wait()
        put_rim(q_raw, 2, h)
        for block in range(BLOCKS):
            row = block * BLOCK
            q_mix[h, pl.ds(row, BLOCK), :] = short(q_raw, 0, h, row, BLOCK).astype(BF16)

    @pl.loop(0, 3)
    def _(i):
        query(i)

    seven = row_in.at[pl.ds(0, ROW - 1)]
    pltpu.make_async_copy(seven, seven, row_recv).wait()
    rate = decays[rr]
    shard = jnp.exp(rate * -float(ROWS))
    whole = jnp.exp(rate * -float(ROWS * ROW))
    total = row_in[0]
    for r in range(1, ROW):
        total = shard * total + row_in[r]
    col_out[...] = total
    col_in[yy] = total

    @pl.loop(1, NSEQ // ROW)
    def _(i):
        pltpu.make_async_remote_copy(
            src_ref=col_out,
            dst_ref=col_in.at[yy],
            send_sem=col_send,
            recv_sem=col_recv,
            device_id=(lax.rem(seq + ROW * i, NSEQ), chan),
            device_id_type=MESH,
        ).start()

    @pl.loop(3, 6)
    def _(i):
        query(i)

    three = col_in.at[pl.ds(0, NSEQ // ROW - 1)]
    pltpu.make_async_copy(three, three, col_recv).wait()
    before = jnp.zeros((MODES, WIDE), F32)
    for y in range(NSEQ // ROW - 1):
        before = jnp.where(y < yy, whole * before + col_in[y], before)
    for r in range(ROW):
        seven_out = local
        if r == 0:
            pltpu.make_async_copy(seven, seven, local_send).wait()
        seven_out[r] = before
        before = shard * before + row_in[r]

    @pl.loop(0, ROW)
    def _(r):
        @pl.when(r == rr)
        def _():
            state[rr] = local[r]

        @pl.when(r != rr)
        def _():
            pltpu.make_async_remote_copy(
                src_ref=local.at[r],
                dst_ref=state.at[rr],
                send_sem=state_send,
                recv_sem=state_recv,
                device_id=(yy * ROW + r, chan),
                device_id_type=MESH,
            ).start()

    @pl.loop(6, HEADS)
    def _(i):
        query(i)

    pltpu.make_async_copy(seven, seven, state_recv).wait()

    @pl.loop(0, HEADS)
    def _(i):
        h = lax.rem(first + i, HEADS)
        step = jnp.exp(decays[h] * -float(BLOCK))
        here = state[h]
        for block in range(BLOCKS):
            rows = pl.ds(block * BLOCK, BLOCK)
            g = gated[h, rows, :]
            high, low = split(here)
            rest = jnp.zeros((BLOCK - 3 * MODES, WIDE), BF16)
            stacked = jnp.concatenate([high, high, low, rest], axis=0)
            conv = matmul(toeplitz[h], jnp.concatenate([g, g], axis=0))
            conv = conv + matmul(from_state[h], stacked)
            m = q_mix[h, rows, :].astype(F32) * conv
            mixed[h, :, rows] = m.T.astype(BF16)
            if block < BLOCKS - 1:
                here = step * here + part[h, block]

        @pl.loop(0, WIDE // SUB)
        def _(n):
            sub = lax.rem(n + seq, WIDE // SUB)
            j = (WIDE // SUB) * h + sub
            source = mixed.at[h, pl.ds(pl.multiple_of(sub * SUB, SUB), SUB), :]

            @pl.when(j == seq)
            def _():
                pltpu.make_async_copy(source, middle.at[seq], a_recv.at[seq]).start()

            @pl.when(j != seq)
            def _():
                pltpu.make_async_remote_copy(
                    src_ref=source,
                    dst_ref=middle.at[seq],
                    send_sem=a_send,
                    recv_sem=a_recv.at[seq],
                    device_id=(j, chan),
                    device_id_type=MESH,
                ).start()

    @pl.loop(0, HEADS)
    def _(i):
        r = residue_of(lax.rem(seq // 4 - i + HEADS, HEADS), chan)
        parity = r // 4

        @pl.loop(0, NSEQ // ROW)
        def _(n):
            y = lax.rem(n + (chan - parity + 1) // 2, NSEQ // ROW)
            source = ROW * y + r
            plane = source // 4
            tokens = pl.multiple_of(lax.rem(source, 4) * ROWS, ROWS)
            place = out_ref.at[chan, :, pl.ds(tokens, ROWS)]
            block = middle.at[source]
            pltpu.make_async_copy(block, block, a_recv.at[source]).wait()

            @pl.when(plane == chan)
            def _():
                pltpu.make_async_copy(block, place, b_recv).start()

            @pl.when(plane != chan)
            def _():
                pltpu.make_async_remote_copy(
                    src_ref=block,
                    dst_ref=place,
                    send_sem=b_send,
                    recv_sem=b_recv,
                    device_id=(seq, plane),
                    device_id_type=MESH,
                ).start()

    three_out = col_in.at[pl.ds(0, NSEQ // ROW - 1)]
    pltpu.make_async_copy(three_out, three_out, col_send).wait()
    pltpu.make_async_copy(seven, seven, state_send).wait()
    sent = middle.at[pl.ds(0, NSEQ - 1)]
    pltpu.make_async_copy(sent, sent, a_send).wait()
    sent = middle.at[pl.ds(0, NSEQ - NSEQ // NCHAN)]
    pltpu.make_async_copy(sent, sent, b_send).wait()
    pltpu.make_async_copy(out_ref, out_ref, b_recv).wait()


def per_device(q_proj, k_proj, v_proj, short_filter, decay_rate, residue):
    dma = pltpu.SemaphoreType.DMA
    out = pl.pallas_call(
        kernel,
        out_shape=jax.ShapeDtypeStruct((NCHAN, SUB, 4 * ROWS), BF16),
        in_specs=[pl.BlockSpec(memory_space=pl.ANY)] * 3
        + [pl.BlockSpec(memory_space=pltpu.VMEM)] * 3,
        out_specs=pl.BlockSpec(memory_space=pl.ANY),
        scratch_shapes=[
            pltpu.VMEM((HEADS, PAD + ROWS, WIDE), BF16),
            pltpu.VMEM((HEADS, PAD + ROWS, WIDE), BF16),
            pltpu.VMEM((HEADS, PAD + ROWS, WIDE), BF16),
            pltpu.VMEM((3, PAD, HEADS * WIDE), BF16),
            pltpu.VMEM((HEADS, ROWS, WIDE), BF16),
            pltpu.VMEM((HEADS, ROWS, WIDE), BF16),
            pltpu.VMEM((HEADS, BLOCK, 2 * BLOCK), BF16),
            pltpu.VMEM((HEADS, BLOCK, BLOCK), BF16),
            pltpu.VMEM((HEADS, 2 * MODES, BLOCK), BF16),
            pltpu.VMEM((HEADS, MODES, WIDE), F32),
            pltpu.VMEM((HEADS, BLOCKS, MODES, WIDE), F32),
            pltpu.VMEM((HEADS, MODES, WIDE), F32),
            pltpu.VMEM((ROW, MODES, WIDE), F32),
            pltpu.VMEM((NSEQ // ROW, MODES, WIDE), F32),
            pltpu.VMEM((MODES, WIDE), F32),
            pltpu.VMEM((HEADS, MODES, WIDE), F32),
            pltpu.VMEM((HEADS, WIDE, ROWS), BF16),
            pltpu.VMEM((NSEQ, SUB, ROWS), BF16),
            dma((HEADS,)), dma((HEADS,)), dma((HEADS,)),
            dma((3,)), dma((3,)),
            dma, dma, dma, dma, dma, dma,
            dma, dma((NSEQ,)), dma, dma,
        ],
        compiler_params=pltpu.CompilerParams(
            collective_id=0, has_side_effects=True, vmem_limit_bytes=56 << 20
        ),
        name="hyena",
    )(q_proj, k_proj, v_proj, short_filter, decay_rate, residue)
    return out[None]


def solution(mesh):
    in_specs = (
        P("seq", "chan"),
        P("seq", "chan"),
        P("seq", "chan"),
        P(None, None, "chan"),
        P("chan", None),
        P("chan", None),
    )
    out_specs = P("seq", None, None, "chan")
    return jax.shard_map(
        per_device, mesh=mesh, in_specs=in_specs, out_specs=out_specs, check_vma=False
    )
```

time: 666 us -> 87.4 us (0.13)
  other arithmetic: 197 us -> 0 us
  starting transfers between devices: 180 us -> 0 us
  blocking collectives: 118 us -> 0 us
  local copies, waits for them, and re-layouts: 105 us -> 3.13 us
  Pallas kernels: 0 us -> 83.9 us
  waiting for transfers between devices: 40.5 us -> 0 us
  matrix products: 21.5 us -> 0 us
    unnamed x2 -> x0, other arithmetic: 182 us -> none
    ppermute x34 -> x0, starting transfers between devices: 180 us -> none  [passed_along(): return lax.ppermute(block, axis, route)]
    all_to_all x2 -> x0, blocking collectives: 118 us -> none  [the longest x1 60 us: per_device(): lax.all_to_all(blocks, 'seq', split_axis=0, concat_axis=3, tiled=True)]
    pallas_call x0 -> x1, Pallas kernels: none -> 83.9 us  [per_device(): pl.pallas_call(kernel, out_shape=jax.ShapeDtypeStruct((NCHAN, SUB, 4 * RO...]
    all_to_all x4 -> x0, local copies, waits for them, and re-layouts: 57.9 us -> none  [the longest x2 32.5 us: per_device(): lax.all_to_all(lax.all_to_all(blocks, 'seq', split_axis=0, concat_axis=3,...]
    ppermute x34 -> x0, waiting for transfers between devices: 40.5 us -> none  [passed_along(): return lax.ppermute(block, axis, route)]
    unnamed x10 -> x1, local copies, waits for them, and re-layouts: 25.2 us -> 3.13 us
    dot_general x17 -> x0, matrix products: 21.5 us -> none  [the longest x8 15 us: advance(): jnp.einsum('htk,khc->thc', kernel_aug, stacked, precision=lax.Precision.H...]
  transfers between devices with their start and end apart: 34 -> 0, of which waited for: 31 -> 0; matrix products, arithmetic and copies ran while one was open for 8% -> 0% of each run, Pallas kernels for 0% -> 0%
where the time goes in v1:
time: 87.4 us; the launch traced here: 87 us
  Pallas kernels  83.9 us (96%)
  local copies, waits for them, and re-layouts  3.13 us (4%)
    pallas_call x1, Pallas kernels, per_device(): pl.pallas_call(kernel, out_shape=jax.ShapeDtypeStruct((NCHAN, SUB, 4 * RO...  83.9 us
    unnamed x1, local copies, waits for them, and re-layouts  3.13 us

profile of v1, /device:TPU:1, one launch (start us, length us, event | category | flops | bytes accessed | tf_op | source)
XLA Modules:
  0.0 87.0 jit_solution(5171359178832932913)
XLA Ops:
  0.0 83.9 %hyena.1 = bf16[8,32,4096]{2,1,0:T(8,128)(2,1)} custom-call(bf16[1024,1024]{1,0:T(8,128)(2,1)} %q_ref.1, bf16[1024,1024]{1,0:T(8,128)(2,1)} %k_ref.1, bf16[1024,1024]{1,0:T(8,128)(2,1)} %v_ref.1, f32[3,3,1024]{2,1,0:T(4,128)} %taps_ref.1, f32[8,16]{1,0:T(8,128)} %decay_ref.1, f32[8,16]{1,0:T(8,128)} %residue_ref.1), custom_call_target="tpu_custom_call" | custom-call | tf_op jit(solution)/shard_map/hyena/pallas_call | solution.py:345
  83.9 3.1 %copy.8 = bf16[1,8,32,4096]{3,2,1,0:T(8,128)(2,1)} copy(bf16[1,8,32,4096]{3,2,1,0:T(8,128)(2,1)} %bitcast.1) | data formatting | bytes 4194304

commit v2 on v1

v2 whole, which is shorter than its diff:
```python
import functools

import jax
import jax.numpy as jnp
from jax import lax
from jax.experimental import pallas as pl
from jax.experimental.pallas import tpu as pltpu
from jax.sharding import PartitionSpec as P

MESH = pl.DeviceIdType.MESH
F32, BF16 = jnp.float32, jnp.bfloat16

ROWS = 1024
HEADS = 8
WIDE = 128
MODES = 16
BLOCK = 128
BLOCKS = ROWS // BLOCK
PAD = 16
NSEQ = 32
NCHAN = 8
SUB = 32
ROW = 8
LOADS = 4
QUERIES = 5
AHEAD = 5


def split(x):
    high = x.astype(BF16)
    return high, (x - high.astype(F32)).astype(BF16)


def matmul(a, b):
    return jnp.dot(a, b, preferred_element_type=F32)


def mod(a, b):
    return lax.rem(a, b)


def kernel(
    q_ref, k_ref, v_ref, taps_in, decay_in, residue_in, out_ref,
    taps_ref, decay_ref, residue_ref,
    q_raw, k_raw, v_raw, gated, q_mix, toeplitz, from_state, into_state,
    decays, part, local, row_in, col_in, col_out, state_out, state, mixed, middle,
    load_q, load_k, load_v, load_p, rim_send, rim_recv,
    local_send, row_recv, col_send, col_recv, state_send, state_recv,
    a_send, a_recv, b_send, b_recv,
):
    seq, chan = lax.axis_index("seq"), lax.axis_index("chan")
    yy, rr = seq // ROW, mod(seq, ROW)

    def columns_of(h):
        return pl.ds(pl.multiple_of(h * WIDE, WIDE), WIDE)

    def load(ref, raw, sem, n, parts):
        width = HEADS * WIDE // parts
        columns = pl.ds(pl.multiple_of(n * width, width), width)
        return pltpu.make_async_copy(
            ref.at[:, columns], raw.at[pl.ds(PAD, ROWS), columns], sem.at[n]
        )

    barrier = pltpu.get_barrier_semaphore()

    def here_for(to_seq, to_chan):
        pl.semaphore_signal(barrier, inc=1, device_id=(to_seq, to_chan), device_id_type=MESH)

    for i in range(1, ROW):
        here_for(yy * ROW + mod(rr + i, ROW), chan)

    @pl.when(jnp.logical_and(rr == 0, yy > 0))
    def _():
        here_for(seq - 1, chan)

    for i in range(1, NSEQ // ROW):
        here_for(mod(seq + i * ROW, NSEQ), chan)

    params = [
        pltpu.make_async_copy(a, b, load_p.at[n])
        for n, (a, b) in enumerate(
            ((taps_in, taps_ref), (decay_in, decay_ref), (residue_in, residue_ref))
        )
    ]
    for copy in params:
        copy.start()
    for n in range(LOADS):
        load(k_ref, k_raw, load_k, n, LOADS).start()
        load(v_ref, v_raw, load_v, n, LOADS).start()
    load(q_ref, q_raw, load_q, 0, 1).start()
    for i in range(1, NCHAN):
        here_for(seq, mod(chan + i, NCHAN))
    for copy in params:
        copy.wait()

    ones_at = lax.broadcasted_iota(jnp.int32, (MODES, MODES), 0) == lax.broadcasted_iota(
        jnp.int32, (MODES, MODES), 1
    )
    lane = lax.broadcasted_iota(jnp.int32, (MODES, BLOCK), 1)
    causal = lax.broadcasted_iota(jnp.int32, (BLOCK, BLOCK), 0) >= lax.broadcasted_iota(
        jnp.int32, (BLOCK, BLOCK), 1
    )

    def column(row):
        wide = jnp.where(ones_at, jnp.broadcast_to(row, (MODES, MODES)), 0.0)
        return jnp.broadcast_to(jnp.sum(wide, axis=1, keepdims=True), (MODES, WIDE))

    for h in range(HEADS):
        rate = column(decay_ref[h : h + 1, :])
        decays[h] = rate
        high, low = split(jnp.exp(-rate * (BLOCK - 1 - lane).astype(F32)))
        into_state[h, 0:MODES] = high
        into_state[h, MODES : 2 * MODES] = low

    def filters(h):
        rate = decays[h]
        weight = column(residue_ref[pl.ds(h, 1), :])
        lag = jnp.where(lane == 0, 0, BLOCK - lane).astype(F32)
        first = jnp.sum(weight * jnp.exp(-rate * lag), axis=0, keepdims=True)
        turned = pltpu.roll(
            jnp.broadcast_to(first, (BLOCK, BLOCK)), 0, 1, stride=1, stride_axis=0
        )
        high, low = split(jnp.where(causal, turned, 0.0))
        toeplitz[h, :, 0:BLOCK] = high
        toeplitz[h, :, BLOCK : 2 * BLOCK] = low
        high, low = split(weight * jnp.exp(-rate * (lane + 1).astype(F32)))
        high, low = high.astype(F32), low.astype(F32)
        rest = jnp.zeros((BLOCK - 3 * MODES, BLOCK), F32)
        from_state[h] = jnp.concatenate([high, low, high, rest], axis=0).T.astype(BF16)

    def taps_of(raw, branch, h, start, count):
        columns = columns_of(h)
        x = raw[pl.ds(start, count), columns].astype(F32)
        y = taps_ref[branch, 0:1, columns] * x
        y = y + taps_ref[branch, 1:2, columns] * pltpu.roll(x, 1, 0)
        return y + taps_ref[branch, 2:3, columns] * pltpu.roll(x, 2, 0)

    def short(raw, branch, h, row, count):
        return taps_of(raw, branch, h, row, count + PAD)[PAD:]

    inner = lax.broadcasted_iota(jnp.int32, (BLOCK, WIDE), 0) >= 2

    def gate(h, block):
        row = block * BLOCK
        if block:
            g = short(k_raw, 1, h, row, BLOCK) * short(v_raw, 2, h, row, BLOCK)
        else:
            g = taps_of(k_raw, 1, h, PAD, BLOCK) * taps_of(v_raw, 2, h, PAD, BLOCK)
            g = jnp.where(inner, g, 0.0)
        g = g.astype(BF16)
        gated[h, pl.ds(row, BLOCK), :] = g
        both = matmul(into_state[h], g)
        both = both[0:MODES] + both[MODES : 2 * MODES]
        part[h, block] = both
        return both

    def gates(n):
        load(k_ref, k_raw, load_k, n, LOADS).wait()
        load(v_ref, v_raw, load_v, n, LOADS).wait()
        for k in range(HEADS // LOADS):
            h = n * (HEADS // LOADS) + k
            step = jnp.exp(decays[h] * -float(BLOCK))
            total = gate(h, 0)
            for block in range(1, BLOCKS):
                total = step * total + gate(h, block)
            local[h] = total

    @pl.loop(0, LOADS // 2)
    def _(n):
        gates(n)

    ends_row = jnp.logical_and(rr == ROW - 1, yy < NSEQ // ROW - 1)
    greeted = ROW - 1 + NSEQ // ROW - 1 + NCHAN - 1

    @pl.when(ends_row)
    def _():
        pl.semaphore_wait(barrier, greeted + 1)

    @pl.when(jnp.logical_not(ends_row))
    def _():
        pl.semaphore_wait(barrier, greeted)

    def rim(n):
        ref, raw = ((k_ref, k_raw), (v_ref, v_raw), (q_ref, q_raw))[n]
        return pltpu.make_async_remote_copy(
            src_ref=ref.at[pl.ds(ROWS - PAD, PAD), :],
            dst_ref=raw.at[pl.ds(0, PAD), :],
            send_sem=rim_send.at[n],
            recv_sem=rim_recv.at[n],
            device_id=(mod(seq + 1, NSEQ), chan),
            device_id_type=MESH,
        )

    @pl.when(seq < NSEQ - 1)
    def _():
        for n in range(3):
            rim(n).start()

    @pl.when(seq == 0)
    def _():
        for raw in (k_raw, v_raw, q_raw):
            raw[0:PAD, :] = jnp.zeros((PAD, HEADS * WIDE), BF16)

    @pl.loop(LOADS // 2, LOADS)
    def _(n):
        gates(n)

    @pl.when(seq > 0)
    def _():
        for n in range(2):
            rim(n).wait_recv()

    firsts = []
    for h in range(HEADS):
        g = taps_of(k_raw, 1, h, 0, 2 * PAD) * taps_of(v_raw, 2, h, 0, 2 * PAD)
        g = g[PAD:].astype(BF16)
        gated[h, 0:PAD, :] = g
        g = g.astype(F32)[0:2]
        firsts.append(g)
        rate = decays[h]
        local[h] = (
            local[h]
            + jnp.exp(rate * -float(ROWS - 1)) * g[0:1]
            + jnp.exp(rate * -float(ROWS - 2)) * g[1:2]
        )
    row_in[rr] = local[rr]

    for i in range(1, ROW):
        h = mod(rr + i, ROW)
        pltpu.make_async_remote_copy(
            src_ref=local.at[h],
            dst_ref=row_in.at[rr],
            send_sem=local_send,
            recv_sem=row_recv,
            device_id=(yy * ROW + h, chan),
            device_id_type=MESH,
        ).start()

    for h in range(HEADS):
        g, rate = firsts[h], decays[h]
        part[h, 0] = (
            part[h, 0]
            + jnp.exp(rate * -float(BLOCK - 1)) * g[0:1]
            + jnp.exp(rate * -float(BLOCK - 2)) * g[1:2]
        )

    @pl.loop(0, HEADS)
    def _(h):
        filters(h)

    load(q_ref, q_raw, load_q, 0, 1).wait()

    @pl.when(seq > 0)
    def _():
        rim(2).wait_recv()

    side, core, half = mod(rr // 2, 2), mod(rr, 2), rr // 4
    parity = mod(half + chan, 2)
    base = 2 * (side + 2 * core) + parity + 2 * yy - 2 * ((chan + parity) // 2) + 2 * NCHAN

    def group_of(i):
        return mod(base + i, HEADS)

    def source_of(i, a, b):
        odd = mod(seq // 4 - i + HEADS, 2)
        turn = mod(seq // 4 - i - odd + HEADS, HEADS) // 2
        s, c = mod(side + a, 2), mod(core + b, 2)
        y = mod(turn - s - 2 * c + (chan + odd) // 2 + NSEQ // ROW, NSEQ // ROW)
        return ROW * y + 4 * mod(odd + chan, 2) + 2 * s + c

    def query(i):
        h = group_of(i)
        for block in range(BLOCKS):
            row = block * BLOCK
            q_mix[h, pl.ds(row, BLOCK), :] = short(q_raw, 0, h, row, BLOCK).astype(BF16)

    seven = row_in.at[pl.ds(0, ROW - 1)]
    three = col_in.at[pl.ds(0, NSEQ // ROW - 1)]
    pltpu.make_async_copy(seven, seven, row_recv).wait()
    rate = decays[rr]
    shard = jnp.exp(rate * -float(ROWS))
    whole = jnp.exp(rate * -float(ROWS * ROW))
    total = row_in[0]
    for r in range(1, ROW):
        total = shard * total + row_in[r]
    col_out[...] = total
    col_in[yy] = total

    for i in range(1, NSEQ // ROW):
        pltpu.make_async_remote_copy(
            src_ref=col_out,
            dst_ref=col_in.at[yy],
            send_sem=col_send,
            recv_sem=col_recv,
            device_id=(mod(seq + ROW * i, NSEQ), chan),
            device_id_type=MESH,
        ).start()

    @pl.loop(0, QUERIES)
    def _(i):
        query(i)

    pltpu.make_async_copy(three, three, col_recv).wait()
    before = jnp.zeros((MODES, WIDE), F32)
    for y in range(NSEQ // ROW - 1):
        before = jnp.where(y < yy, whole * before + col_in[y], before)
    for r in range(ROW):
        state_out[r] = before
        before = shard * before + row_in[r]
    state[rr] = state_out[rr]

    for i in range(1, ROW):
        r = mod(rr + i, ROW)
        pltpu.make_async_remote_copy(
            src_ref=state_out.at[r],
            dst_ref=state.at[rr],
            send_sem=state_send,
            recv_sem=state_recv,
            device_id=(yy * ROW + r, chan),
            device_id_type=MESH,
        ).start()

    @pl.loop(QUERIES, HEADS)
    def _(i):
        query(i)

    pltpu.make_async_copy(seven, seven, state_recv).wait()

    def mix(i):
        h = group_of(i)
        step = jnp.exp(decays[h] * -float(BLOCK))
        here = state[h]
        for block in range(BLOCKS):
            rows = pl.ds(block * BLOCK, BLOCK)
            g = gated[h, rows, :]
            high, low = split(here)
            rest = jnp.zeros((BLOCK - 3 * MODES, WIDE), BF16)
            stacked = jnp.concatenate([high, high, low, rest], axis=0)
            conv = matmul(toeplitz[h], jnp.concatenate([g, g], axis=0))
            conv = conv + matmul(from_state[h], stacked)
            m = q_mix[h, rows, :].astype(F32) * conv
            mixed[h, :, rows] = m.T.astype(BF16)
            if block < BLOCKS - 1:
                here = step * here + part[h, block]

    def send(i, a, b):
        h = group_of(i)
        sub = 2 * mod(side + a, 2) + mod(core + b, 2)
        j = (WIDE // SUB) * h + sub
        source = mixed.at[h, pl.ds(pl.multiple_of(sub * SUB, SUB), SUB), :]

        @pl.when(j == seq)
        def _():
            pltpu.make_async_copy(source, middle.at[seq], a_recv.at[seq]).start()

        @pl.when(j != seq)
        def _():
            pltpu.make_async_remote_copy(
                src_ref=source,
                dst_ref=middle.at[seq],
                send_sem=a_send,
                recv_sem=a_recv.at[seq],
                device_id=(j, chan),
                device_id_type=MESH,
            ).start()

    def forward(i, a, b):
        source = source_of(i, a, b)
        plane = source // 4
        tokens = pl.multiple_of(mod(source, 4) * ROWS, ROWS)
        place = out_ref.at[chan, :, pl.ds(tokens, ROWS)]
        block = middle.at[source]
        pltpu.make_async_copy(block, block, a_recv.at[source]).wait()

        @pl.when(plane == chan)
        def _():
            pltpu.make_async_copy(block, place, b_recv).start()

        @pl.when(plane != chan)
        def _():
            pltpu.make_async_remote_copy(
                src_ref=block,
                dst_ref=place,
                send_sem=b_send,
                recv_sem=b_recv,
                device_id=(seq, plane),
                device_id_type=MESH,
            ).start()

    def in_order(turn, m):
        turn(m // 4, mod(m // 2, 2), mod(m, 2))

    @pl.loop(0, NSEQ + AHEAD)
    def _(m):
        @pl.when(jnp.logical_and(m < NSEQ, mod(m, 4) == 0))
        def _():
            mix(m // 4)

        @pl.when(m < NSEQ)
        def _():
            in_order(send, m)

        @pl.when(m >= AHEAD)
        def _():
            in_order(forward, m - AHEAD)

    @pl.when(seq < NSEQ - 1)
    def _():
        for n in range(3):
            rim(n).wait_send()

    pltpu.make_async_copy(seven, seven, local_send).wait()
    pltpu.make_async_copy(three, three, col_send).wait()
    pltpu.make_async_copy(seven, seven, state_send).wait()
    sent = middle.at[pl.ds(0, NSEQ - 1)]
    pltpu.make_async_copy(sent, sent, a_send).wait()
    sent = middle.at[pl.ds(0, NSEQ - NSEQ // NCHAN)]
    pltpu.make_async_copy(sent, sent, b_send).wait()
    pltpu.make_async_copy(out_ref, out_ref, b_recv).wait()


def per_device(q_proj, k_proj, v_proj, short_filter, decay_rate, residue):
    dma = pltpu.SemaphoreType.DMA
    raw = pltpu.VMEM((PAD + ROWS, HEADS * WIDE), BF16)
    out = pl.pallas_call(
        kernel,
        out_shape=jax.ShapeDtypeStruct((NCHAN, SUB, 4 * ROWS), BF16),
        in_specs=[pl.BlockSpec(memory_space=pl.ANY)] * 6,
        out_specs=pl.BlockSpec(memory_space=pl.ANY),
        scratch_shapes=[
            pltpu.VMEM(short_filter.shape, F32),
            pltpu.VMEM(decay_rate.shape, F32),
            pltpu.VMEM(residue.shape, F32),
            raw, raw, raw,
            pltpu.VMEM((HEADS, ROWS, WIDE), BF16),
            pltpu.VMEM((HEADS, ROWS, WIDE), BF16),
            pltpu.VMEM((HEADS, BLOCK, 2 * BLOCK), BF16),
            pltpu.VMEM((HEADS, BLOCK, BLOCK), BF16),
            pltpu.VMEM((HEADS, 2 * MODES, BLOCK), BF16),
            pltpu.VMEM((HEADS, MODES, WIDE), F32),
            pltpu.VMEM((HEADS, BLOCKS, MODES, WIDE), F32),
            pltpu.VMEM((HEADS, MODES, WIDE), F32),
            pltpu.VMEM((ROW, MODES, WIDE), F32),
            pltpu.VMEM((NSEQ // ROW, MODES, WIDE), F32),
            pltpu.VMEM((MODES, WIDE), F32),
            pltpu.VMEM((ROW, MODES, WIDE), F32),
            pltpu.VMEM((HEADS, MODES, WIDE), F32),
            pltpu.VMEM((HEADS, WIDE, ROWS), BF16),
            pltpu.VMEM((NSEQ, SUB, ROWS), BF16),
            dma((1,)), dma((LOADS,)), dma((LOADS,)), dma((3,)),
            dma((3,)), dma((3,)),
            dma, dma, dma, dma, dma, dma,
            dma, dma((NSEQ,)), dma, dma,
        ],
        compiler_params=pltpu.CompilerParams(
            collective_id=0, has_side_effects=True, vmem_limit_bytes=56 << 20
        ),
        name="hyena",
    )(q_proj, k_proj, v_proj, short_filter, decay_rate, residue)
    return out[None]


def solution(mesh):
    in_specs = (
        P("seq", "chan"),
        P("seq", "chan"),
        P("seq", "chan"),
        P(None, None, "chan"),
        P("chan", None),
        P("chan", None),
    )
    out_specs = P("seq", None, None, "chan")
    return jax.shard_map(
        per_device, mesh=mesh, in_specs=in_specs, out_specs=out_specs, check_vma=False
    )
```

time: 87.4 us -> 81.3 us (0.930)
  Pallas kernels: 83.9 us -> 77.2 us
    pallas_call x1, Pallas kernels: 83.9 us -> 77.2 us  [per_device(): pl.pallas_call(kernel, out_shape=jax.ShapeDtypeStruct((NCHAN, SUB, 4 * RO...]
where the time goes in v2:
time: 81.3 us; the launch traced here: 80.4 us
  Pallas kernels  77.2 us (95%)
  local copies, waits for them, and re-layouts  3.13 us (4%)
    pallas_call x1, Pallas kernels, per_device(): pl.pallas_call(kernel, out_shape=jax.ShapeDtypeStruct((NCHAN, SUB, 4 * RO...  77.2 us
    unnamed x1, local copies, waits for them, and re-layouts  3.13 us

profile of v2, /device:TPU:1, one launch (start us, length us, event | category | flops | bytes accessed | tf_op | source)
XLA Modules:
  0.0 80.4 jit_solution(5118994319177023129)
XLA Ops:
  0.0 77.2 %hyena.1 = bf16[8,32,4096]{2,1,0:T(8,128)(2,1)} custom-call(bf16[1024,1024]{1,0:T(8,128)(2,1)} %q_ref.1, bf16[1024,1024]{1,0:T(8,128)(2,1)} %k_ref.1, bf16[1024,1024]{1,0:T(8,128)(2,1)} %v_ref.1, f32[3,3,1024]{2,1,0:T(4,128)} %taps_in.1, f32[8,16]{1,0:T(8,128)} %decay_in.1, f32[8,16]{1,0:T(8,128)} %residue_in.1), custom_call_target="tpu_custom_call" | custom-call | tf_op jit(solution)/shard_map/hyena/pallas_call | solution.py:425
  77.2 3.1 %copy.8 = bf16[1,8,32,4096]{3,2,1,0:T(8,128)(2,1)} copy(bf16[1,8,32,4096]{3,2,1,0:T(8,128)(2,1)} %bitcast.1) | data formatting | bytes 4194304

commit v3 on v2

--- a/solution.py
+++ b/solution.py
@@ -22,7 +22,9 @@
 SUB = 32
 ROW = 8
 LOADS = 4
-QUERIES = 5
+FILTERS = 1
+QUERIES = 2
+MORE = 5
 AHEAD = 5
 
 
@@ -40,11 +42,10 @@
 
 
 def kernel(
-    q_ref, k_ref, v_ref, taps_in, decay_in, residue_in, out_ref,
-    taps_ref, decay_ref, residue_ref,
+    q_ref, k_ref, v_ref, params_ref, out_ref,
     q_raw, k_raw, v_raw, gated, q_mix, toeplitz, from_state, into_state,
-    decays, part, local, row_in, col_in, col_out, state_out, state, mixed, middle,
-    load_q, load_k, load_v, load_p, rim_send, rim_recv,
+    decays, first_on, part, local, row_in, col_in, col_out, state_out, state, mixed, middle,
+    load_q, load_k, load_v, rim_send, rim_recv,
     local_send, row_recv, col_send, col_recv, state_send, state_recv,
     a_send, a_recv, b_send, b_recv,
 ):
@@ -61,11 +62,16 @@
             ref.at[:, columns], raw.at[pl.ds(PAD, ROWS), columns], sem.at[n]
         )
 
+    load(k_ref, k_raw, load_k, 0, LOADS).start()
+    load(v_ref, v_raw, load_v, 0, LOADS).start()
+
     barrier = pltpu.get_barrier_semaphore()
 
     def here_for(to_seq, to_chan):
         pl.semaphore_signal(barrier, inc=1, device_id=(to_seq, to_chan), device_id_type=MESH)
 
+    for i in range(1, NCHAN):
+        here_for(seq, mod(chan + i, NCHAN))
     for i in range(1, ROW):
         here_for(yy * ROW + mod(rr + i, ROW), chan)
 
@@ -76,22 +82,10 @@
     for i in range(1, NSEQ // ROW):
         here_for(mod(seq + i * ROW, NSEQ), chan)
 
-    params = [
-        pltpu.make_async_copy(a, b, load_p.at[n])
-        for n, (a, b) in enumerate(
-            ((taps_in, taps_ref), (decay_in, decay_ref), (residue_in, residue_ref))
-        )
-    ]
-    for copy in params:
-        copy.start()
-    for n in range(LOADS):
+    for n in range(1, LOADS):
         load(k_ref, k_raw, load_k, n, LOADS).start()
         load(v_ref, v_raw, load_v, n, LOADS).start()
     load(q_ref, q_raw, load_q, 0, 1).start()
-    for i in range(1, NCHAN):
-        here_for(seq, mod(chan + i, NCHAN))
-    for copy in params:
-        copy.wait()
 
     ones_at = lax.broadcasted_iota(jnp.int32, (MODES, MODES), 0) == lax.broadcasted_iota(
         jnp.int32, (MODES, MODES), 1
@@ -106,15 +100,17 @@
         return jnp.broadcast_to(jnp.sum(wide, axis=1, keepdims=True), (MODES, WIDE))
 
     for h in range(HEADS):
-        rate = column(decay_ref[h : h + 1, :])
+        rate = column(params_ref[3, h : h + 1, 0:MODES])
         decays[h] = rate
+        first_on[h, 0] = jnp.exp(rate * -float(ROWS - 1))
+        first_on[h, 1] = jnp.exp(rate * -float(ROWS - 2))
         high, low = split(jnp.exp(-rate * (BLOCK - 1 - lane).astype(F32)))
         into_state[h, 0:MODES] = high
         into_state[h, MODES : 2 * MODES] = low
 
     def filters(h):
         rate = decays[h]
-        weight = column(residue_ref[pl.ds(h, 1), :])
+        weight = column(params_ref[4, h : h + 1, 0:MODES])
         lag = jnp.where(lane == 0, 0, BLOCK - lane).astype(F32)
         first = jnp.sum(weight * jnp.exp(-rate * lag), axis=0, keepdims=True)
         turned = pltpu.roll(
@@ -131,9 +127,9 @@
     def taps_of(raw, branch, h, start, count):
         columns = columns_of(h)
         x = raw[pl.ds(start, count), columns].astype(F32)
-        y = taps_ref[branch, 0:1, columns] * x
-        y = y + taps_ref[branch, 1:2, columns] * pltpu.roll(x, 1, 0)
-        return y + taps_ref[branch, 2:3, columns] * pltpu.roll(x, 2, 0)
+        y = params_ref[branch, 0:1, columns] * x
+        y = y + params_ref[branch, 1:2, columns] * pltpu.roll(x, 1, 0)
+        return y + params_ref[branch, 2:3, columns] * pltpu.roll(x, 2, 0)
 
     def short(raw, branch, h, row, count):
         return taps_of(raw, branch, h, row, count + PAD)[PAD:]
@@ -154,9 +150,11 @@
         part[h, block] = both
         return both
 
-    def gates(n):
+    def loaded(n):
         load(k_ref, k_raw, load_k, n, LOADS).wait()
         load(v_ref, v_raw, load_v, n, LOADS).wait()
+
+    def gates(n):
         for k in range(HEADS // LOADS):
             h = n * (HEADS // LOADS) + k
             step = jnp.exp(decays[h] * -float(BLOCK))
@@ -165,9 +163,10 @@
                 total = step * total + gate(h, block)
             local[h] = total
 
-    @pl.loop(0, LOADS // 2)
-    def _(n):
-        gates(n)
+    loaded(0)
+    gates(0)
+    for n in range(1, LOADS):
+        loaded(n)
 
     ends_row = jnp.logical_and(rr == ROW - 1, yy < NSEQ // ROW - 1)
     greeted = ROW - 1 + NSEQ // ROW - 1 + NCHAN - 1
@@ -181,9 +180,9 @@
         pl.semaphore_wait(barrier, greeted)
 
     def rim(n):
-        ref, raw = ((k_ref, k_raw), (v_ref, v_raw), (q_ref, q_raw))[n]
+        raw = (k_raw, v_raw, q_raw)[n]
         return pltpu.make_async_remote_copy(
-            src_ref=ref.at[pl.ds(ROWS - PAD, PAD), :],
+            src_ref=raw.at[pl.ds(ROWS, PAD), :],
             dst_ref=raw.at[pl.ds(0, PAD), :],
             send_sem=rim_send.at[n],
             recv_sem=rim_recv.at[n],
@@ -193,7 +192,7 @@
 
     @pl.when(seq < NSEQ - 1)
     def _():
-        for n in range(3):
+        for n in range(2):
             rim(n).start()
 
     @pl.when(seq == 0)
@@ -201,7 +200,7 @@
         for raw in (k_raw, v_raw, q_raw):
             raw[0:PAD, :] = jnp.zeros((PAD, HEADS * WIDE), BF16)
 
-    @pl.loop(LOADS // 2, LOADS)
+    @pl.loop(1, LOADS)
     def _(n):
         gates(n)
 
@@ -217,12 +216,7 @@
         gated[h, 0:PAD, :] = g
         g = g.astype(F32)[0:2]
         firsts.append(g)
-        rate = decays[h]
-        local[h] = (
-            local[h]
-            + jnp.exp(rate * -float(ROWS - 1)) * g[0:1]
-            + jnp.exp(rate * -float(ROWS - 2)) * g[1:2]
-        )
+        local[h] = local[h] + first_on[h, 0] * g[0:1] + first_on[h, 1] * g[1:2]
     row_in[rr] = local[rr]
 
     for i in range(1, ROW):
@@ -236,6 +230,12 @@
             device_id_type=MESH,
         ).start()
 
+    load(q_ref, q_raw, load_q, 0, 1).wait()
+
+    @pl.when(seq < NSEQ - 1)
+    def _():
+        rim(2).start()
+
     for h in range(HEADS):
         g, rate = firsts[h], decays[h]
         part[h, 0] = (
@@ -244,19 +244,9 @@
             + jnp.exp(rate * -float(BLOCK - 2)) * g[1:2]
         )
 
-    @pl.loop(0, HEADS)
-    def _(h):
-        filters(h)
-
-    load(q_ref, q_raw, load_q, 0, 1).wait()
-
-    @pl.when(seq > 0)
-    def _():
-        rim(2).wait_recv()
-
     side, core, half = mod(rr // 2, 2), mod(rr, 2), rr // 4
     parity = mod(half + chan, 2)
-    base = 2 * (side + 2 * core) + parity + 2 * yy - 2 * ((chan + parity) // 2) + 2 * NCHAN
+    base = 2 * (1 - side + 2 * core) + parity + 2 * yy - 2 * ((chan + parity) // 2) + 2 * NCHAN
 
     def group_of(i):
         return mod(base + i, HEADS)
@@ -265,7 +255,7 @@
         odd = mod(seq // 4 - i + HEADS, 2)
         turn = mod(seq // 4 - i - odd + HEADS, HEADS) // 2
         s, c = mod(side + a, 2), mod(core + b, 2)
-        y = mod(turn - s - 2 * c + (chan + odd) // 2 + NSEQ // ROW, NSEQ // ROW)
+        y = mod(turn - (1 - s) - 2 * c + (chan + odd) // 2 + NSEQ // ROW, NSEQ // ROW)
         return ROW * y + 4 * mod(odd + chan, 2) + 2 * s + c
 
     def query(i):
@@ -273,6 +263,9 @@
         for block in range(BLOCKS):
             row = block * BLOCK
             q_mix[h, pl.ds(row, BLOCK), :] = short(q_raw, 0, h, row, BLOCK).astype(BF16)
+
+    for h in range(FILTERS):
+        filters(h)
 
     seven = row_in.at[pl.ds(0, ROW - 1)]
     three = col_in.at[pl.ds(0, NSEQ // ROW - 1)]
@@ -296,6 +289,13 @@
             device_id_type=MESH,
         ).start()
 
+    for h in range(FILTERS, HEADS):
+        filters(h)
+
+    @pl.when(seq > 0)
+    def _():
+        rim(2).wait_recv()
+
     @pl.loop(0, QUERIES)
     def _(i):
         query(i)
@@ -320,13 +320,17 @@
             device_id_type=MESH,
         ).start()
 
-    @pl.loop(QUERIES, HEADS)
+    @pl.loop(QUERIES, MORE)
     def _(i):
         query(i)
 
     pltpu.make_async_copy(seven, seven, state_recv).wait()
 
     def mix(i):
+        @pl.when(i >= MORE)
+        def _():
+            query(i)
+
         h = group_of(i)
         step = jnp.exp(decays[h] * -float(BLOCK))
         here = state[h]
@@ -421,16 +425,21 @@
 
 def per_device(q_proj, k_proj, v_proj, short_filter, decay_rate, residue):
     dma = pltpu.SemaphoreType.DMA
+    beside = ((0, 0), (0, 0), (0, HEADS * WIDE - MODES))
+    params = jnp.concatenate(
+        [
+            jnp.pad(short_filter, ((0, 0), (0, HEADS - 3), (0, 0))),
+            jnp.pad(decay_rate[None], beside),
+            jnp.pad(residue[None], beside),
+        ]
+    )
     raw = pltpu.VMEM((PAD + ROWS, HEADS * WIDE), BF16)
     out = pl.pallas_call(
         kernel,
         out_shape=jax.ShapeDtypeStruct((NCHAN, SUB, 4 * ROWS), BF16),
-        in_specs=[pl.BlockSpec(memory_space=pl.ANY)] * 6,
+        in_specs=[pl.BlockSpec(memory_space=pl.ANY)] * 3 + [pl.BlockSpec(memory_space=pltpu.VMEM)],
         out_specs=pl.BlockSpec(memory_space=pl.ANY),
         scratch_shapes=[
-            pltpu.VMEM(short_filter.shape, F32),
-            pltpu.VMEM(decay_rate.shape, F32),
-            pltpu.VMEM(residue.shape, F32),
             raw, raw, raw,
             pltpu.VMEM((HEADS, ROWS, WIDE), BF16),
             pltpu.VMEM((HEADS, ROWS, WIDE), BF16),
@@ -438,6 +447,7 @@
             pltpu.VMEM((HEADS, BLOCK, BLOCK), BF16),
             pltpu.VMEM((HEADS, 2 * MODES, BLOCK), BF16),
             pltpu.VMEM((HEADS, MODES, WIDE), F32),
+            pltpu.VMEM((HEADS, 2, MODES, WIDE), F32),
             pltpu.VMEM((HEADS, BLOCKS, MODES, WIDE), F32),
             pltpu.VMEM((HEADS, MODES, WIDE), F32),
             pltpu.VMEM((ROW, MODES, WIDE), F32),
@@ -447,16 +457,16 @@
             pltpu.VMEM((HEADS, MODES, WIDE), F32),
             pltpu.VMEM((HEADS, WIDE, ROWS), BF16),
             pltpu.VMEM((NSEQ, SUB, ROWS), BF16),
-            dma((1,)), dma((LOADS,)), dma((LOADS,)), dma((3,)),
+            dma((1,)), dma((LOADS,)), dma((LOADS,)),
             dma((3,)), dma((3,)),
             dma, dma, dma, dma, dma, dma,
             dma, dma((NSEQ,)), dma, dma,
         ],
         compiler_params=pltpu.CompilerParams(
-            collective_id=0, has_side_effects=True, vmem_limit_bytes=56 << 20
+            collective_id=0, has_side_effects=True, vmem_limit_bytes=50 << 20
         ),
         name="hyena",
-    )(q_proj, k_proj, v_proj, short_filter, decay_rate, residue)
+    )(q_proj, k_proj, v_proj, params)
     return out[None]
 
 

time: 81.3 us -> 79.5 us (0.978)
  local copies, waits for them, and re-layouts: 3.13 us -> 1.32 us
  other arithmetic: 0 us -> 0.84 us
    unnamed x1, local copies, waits for them, and re-layouts: 3.13 us -> 1.32 us
    concatenate x0 -> x1, other arithmetic: none -> 0.84 us  [per_device(): jnp.concatenate([jnp.pad(short_filter, ((0, 0), (0, HEADS - 3), (0, 0))),...]
where the time goes in v3:
time: 79.5 us; the launch traced here: 78.7 us
  Pallas kernels  76.5 us (96%)
  local copies, waits for them, and re-layouts  1.32 us (2%)
  other arithmetic  0.84 us (1%)
    pallas_call x1, Pallas kernels, per_device(): pl.pallas_call(kernel, out_shape=jax.ShapeDtypeStruct((NCHAN, SUB, 4 * RO...  76.5 us

profile of v3, /device:TPU:1, one launch (start us, length us, event | category | flops | bytes accessed | tf_op | source)
XLA Modules:
  0.0 78.7 jit_solution(18232979536965111435)
XLA Ops:
  0.0 0.8 %select_maximum_fusion.params_ref = f32[5,8,1024]{2,1,0:T(8,128)S(1)} fusion(f32[1,8,16]{2,1,0:T(8,128)} %bitcast.4, f32[1,8,16]{2,1,0:T(8,128)} %bitcast.5, f32[3,3,1024]{2,1,0:T(4,128)} %param.9), kind=kLoop, calls=%fused_computation.2 | loop fusion | flops 409600 | bytes 201728 | tf_op jit(solution)/shard_map/concatenate | solution.py:429
  0.8 76.5 %hyena.1 = bf16[8,32,4096]{2,1,0:T(8,128)(2,1)S(1)} custom-call(bf16[1024,1024]{1,0:T(8,128)(2,1)} %q_ref.1, bf16[1024,1024]{1,0:T(8,128)(2,1)} %k_ref.1, bf16[1024,1024]{1,0:T(8,128)(2,1)} %v_ref.1, f32[5,8,1024]{2,1,0:T(8,128)S(1)} %select_maximum_fusion.params_ref), custom_call_target="tpu_custom_call" | custom-call | tf_op jit(solution)/shard_map/hyena/pallas_call | solution.py:437
  77.3 1.3 %copy.8 = bf16[1,8,32,4096]{3,2,1,0:T(8,128)(2,1)} copy(bf16[1,8,32,4096]{3,2,1,0:T(8,128)(2,1)S(1)} %bitcast.3) | data formatting | bytes 4194304

commit v4 on v3

--- a/solution.py
+++ b/solution.py
@@ -25,7 +25,7 @@
 FILTERS = 1
 QUERIES = 2
 MORE = 5
-AHEAD = 5
+AHEAD = 4
 
 
 def split(x):
@@ -200,8 +200,7 @@
         for raw in (k_raw, v_raw, q_raw):
             raw[0:PAD, :] = jnp.zeros((PAD, HEADS * WIDE), BF16)
 
-    @pl.loop(1, LOADS)
-    def _(n):
+    for n in range(1, LOADS):
         gates(n)
 
     @pl.when(seq > 0)

time: 79.5 us -> 78.8 us (level)
  no operation moved by 1% of the time
where the time goes in v4:
time: 78.8 us; the launch traced here: 78.7 us
  Pallas kernels  76.5 us (97%)
  local copies, waits for them, and re-layouts  1.32 us (2%)
  other arithmetic  0.84 us (1%)
    pallas_call x1, Pallas kernels, per_device(): pl.pallas_call(kernel, out_shape=jax.ShapeDtypeStruct((NCHAN, SUB, 4 * RO...  76.5 us

profile of v4, /device:TPU:1, one launch (start us, length us, event | category | flops | bytes accessed | tf_op | source)
XLA Modules:
  0.0 78.7 jit_solution(12596783557834759518)
XLA Ops:
  0.0 0.8 %select_maximum_fusion.params_ref = f32[5,8,1024]{2,1,0:T(8,128)S(1)} fusion(f32[1,8,16]{2,1,0:T(8,128)} %bitcast.4, f32[1,8,16]{2,1,0:T(8,128)} %bitcast.5, f32[3,3,1024]{2,1,0:T(4,128)} %param.9), kind=kLoop, calls=%fused_computation.2 | loop fusion | flops 409600 | bytes 201728 | tf_op jit(solution)/shard_map/concatenate | solution.py:428
  0.8 76.5 %hyena.1 = bf16[8,32,4096]{2,1,0:T(8,128)(2,1)S(1)} custom-call(bf16[1024,1024]{1,0:T(8,128)(2,1)} %q_ref.1, bf16[1024,1024]{1,0:T(8,128)(2,1)} %k_ref.1, bf16[1024,1024]{1,0:T(8,128)(2,1)} %v_ref.1, f32[5,8,1024]{2,1,0:T(8,128)S(1)} %select_maximum_fusion.params_ref), custom_call_target="tpu_custom_call" | custom-call | tf_op jit(solution)/shard_map/hyena/pallas_call | solution.py:436
  77.3 1.3 %copy.8 = bf16[1,8,32,4096]{3,2,1,0:T(8,128)(2,1)} copy(bf16[1,8,32,4096]{3,2,1,0:T(8,128)(2,1)S(1)} %bitcast.3) | data formatting | bytes 4194304

commit v5 on v4

--- a/solution.py
+++ b/solution.py
@@ -215,19 +215,23 @@
         gated[h, 0:PAD, :] = g
         g = g.astype(F32)[0:2]
         firsts.append(g)
-        local[h] = local[h] + first_on[h, 0] * g[0:1] + first_on[h, 1] * g[1:2]
-    row_in[rr] = local[rr]
-
-    for i in range(1, ROW):
-        h = mod(rr + i, ROW)
-        pltpu.make_async_remote_copy(
-            src_ref=local.at[h],
-            dst_ref=row_in.at[rr],
-            send_sem=local_send,
-            recv_sem=row_recv,
-            device_id=(yy * ROW + h, chan),
-            device_id_type=MESH,
-        ).start()
+        total = local[h] + first_on[h, 0] * g[0:1] + first_on[h, 1] * g[1:2]
+        local[h] = total
+
+        @pl.when(h == rr)
+        def _():
+            row_in[rr] = total
+
+        @pl.when(h != rr)
+        def _():
+            pltpu.make_async_remote_copy(
+                src_ref=local.at[h],
+                dst_ref=row_in.at[rr],
+                send_sem=local_send,
+                recv_sem=row_recv,
+                device_id=(yy * ROW + h, chan),
+                device_id_type=MESH,
+            ).start()
 
     load(q_ref, q_raw, load_q, 0, 1).wait()
 
@@ -305,19 +309,23 @@
         before = jnp.where(y < yy, whole * before + col_in[y], before)
     for r in range(ROW):
         state_out[r] = before
+
+        @pl.when(r == rr)
+        def _():
+            state[rr] = before
+
+        @pl.when(r != rr)
+        def _():
+            pltpu.make_async_remote_copy(
+                src_ref=state_out.at[r],
+                dst_ref=state.at[rr],
+                send_sem=state_send,
+                recv_sem=state_recv,
+                device_id=(yy * ROW + r, chan),
+                device_id_type=MESH,
+            ).start()
+
         before = shard * before + row_in[r]
-    state[rr] = state_out[rr]
-
-    for i in range(1, ROW):
-        r = mod(rr + i, ROW)
-        pltpu.make_async_remote_copy(
-            src_ref=state_out.at[r],
-            dst_ref=state.at[rr],
-            send_sem=state_send,
-            recv_sem=state_recv,
-            device_id=(yy * ROW + r, chan),
-            device_id_type=MESH,
-        ).start()
 
     @pl.loop(QUERIES, MORE)
     def _(i):

time: 78.8 us -> 78.8 us (level)
  no operation moved by 1% of the time
where the time goes in v5:
time: 78.8 us; the launch traced here: 78.6 us
  Pallas kernels  76.5 us (97%)
  local copies, waits for them, and re-layouts  1.32 us (2%)
  other arithmetic  0.84 us (1%)
    pallas_call x1, Pallas kernels, per_device(): pl.pallas_call(kernel, out_shape=jax.ShapeDtypeStruct((NCHAN, SUB, 4 * RO...  76.5 us

profile of v5, /device:TPU:1, one launch (start us, length us, event | category | flops | bytes accessed | tf_op | source)
XLA Modules:
  0.0 78.6 jit_solution(10142524435813764081)
XLA Ops:
  0.0 0.8 %select_maximum_fusion.params_ref = f32[5,8,1024]{2,1,0:T(8,128)S(1)} fusion(f32[1,8,16]{2,1,0:T(8,128)} %bitcast.4, f32[1,8,16]{2,1,0:T(8,128)} %bitcast.5, f32[3,3,1024]{2,1,0:T(4,128)} %param.9), kind=kLoop, calls=%fused_computation.2 | loop fusion | flops 409600 | bytes 201728 | tf_op jit(solution)/shard_map/concatenate | solution.py:436
  0.8 76.5 %hyena.1 = bf16[8,32,4096]{2,1,0:T(8,128)(2,1)S(1)} custom-call(bf16[1024,1024]{1,0:T(8,128)(2,1)} %q_ref.1, bf16[1024,1024]{1,0:T(8,128)(2,1)} %k_ref.1, bf16[1024,1024]{1,0:T(8,128)(2,1)} %v_ref.1, f32[5,8,1024]{2,1,0:T(8,128)S(1)} %select_maximum_fusion.params_ref), custom_call_target="tpu_custom_call" | custom-call | tf_op jit(solution)/shard_map/hyena/pallas_call | solution.py:444
  77.3 1.3 %copy.8 = bf16[1,8,32,4096]{3,2,1,0:T(8,128)(2,1)} copy(bf16[1,8,32,4096]{3,2,1,0:T(8,128)(2,1)S(1)} %bitcast.3) | data formatting | bytes 4194304
